TPU v7x, 32 devices: a whole 2x2x4 slice. The times are simulated.
32 devices in a mesh: grp: 2 (over y), row: 4 (over z), col: 4 (over x, core).
Axes of the slice: x: 2, y: 2, z: 4, core: 2. Of those that a mesh axis runs over, the one named last changes fastest.
Arguments:
- out_first: float32 [512, 6144], P(('grp', 'col'), 'row'), parts along dimension 0, may hold values from -6 to 6
- out_second: float32 [512, 6144], P(('grp', 'col'), 'row'), parts along dimension 0, may hold values from -6 to 6
- grad_first: float32 [512, 6144], P(('grp', 'col'), 'row'), parts along dimension 0, may hold values from -6 to 6
- grad_second: float32 [512, 6144], P(('grp', 'col'), 'row'), parts along dimension 0, may hold values from -6 to 6
- w_query: bfloat16 [6144, 6144], P('row', 'col'), may hold values from -1 to 1
- w_key: bfloat16 [6144, 6144], P('row', 'col'), may hold values from -1 to 1
- w_value: bfloat16 [6144, 6144], P('row', 'col'), may hold values from -0.078125 to 0.078125
- w_out: bfloat16 [6144, 6144], P('col', 'row'), may hold values from -0.078125 to 0.078125
- w_up: bfloat16 [6144, 24576], P('row', 'col'), may hold values from -0.078125 to 0.078125
- w_down: bfloat16 [24576, 6144], P('col', 'row'), may hold values from -0.0390625 to 0.0390625
Outputs:
- input_first: float32 [512, 6144], P(('grp', 'col'), 'row'), parts along dimension 0
- input_second: float32 [512, 6144], P(('grp', 'col'), 'row'), parts along dimension 0
- grad_input_first: float32 [512, 6144], P(('grp', 'col'), 'row'), parts along dimension 0
- grad_input_second: float32 [512, 6144], P(('grp', 'col'), 'row'), parts along dimension 0
- grad_up: bfloat16 [12288, 24576], P(('grp', 'row'), 'col'), parts along dimension 0
- grad_down: bfloat16 [49152, 6144], P(('grp', 'col'), 'row'), parts along dimension 0
There are 2 independent parts, one for each index of `grp`. A program takes and returns all parts, laid end to end along the dimension named above; an argument that names none is the same for every part. Nothing has to cross between parts.
All inputs are finite; a program needn't handle non-finite values.
Results may differ from a plain program's by a relative error of at most 0.04.
Values may be sent and summed in bfloat16 or wider, within the bound.
A program may use at most 256 MiB of HBM per device.

v0:
```python
import math

import jax
import jax.numpy as jnp
from jax import lax
from jax.sharding import PartitionSpec as P

HEAD = 128


def for_sending(array):
    return jax.tree.map(lambda a: a.astype(jnp.bfloat16) if a.dtype == jnp.float32 else a, array)


def tanh_gelu(pre):
    inner = 0.7978845608028654 * (pre + 0.044715 * pre * pre * pre)
    slopes = jnp.tanh(inner)
    act_value = 0.5 * pre * (1.0 + slopes)
    change = 0.5 * (1.0 + slopes) + 0.5 * pre * (1.0 - slopes * slopes) * 0.7978845608028654 * (
        1.0 + 3.0 * 0.044715 * pre * pre
    )
    return (act_value, change)


def times_trans(first_op, second_op):
    return lax.dot_general(
        first_op, second_op, (((1,), (1,)), ((), ())), preferred_element_type=jnp.float32
    )


def trans_times(first_op, second_op):
    return lax.dot_general(
        first_op, second_op, (((0,), (0,)), ((), ())), preferred_element_type=jnp.float32
    )


def col_panels(arrays):
    return (
        lax.all_gather(arrays[0], "col", axis=0, tiled=True),
        lax.all_gather(arrays[1], "col", axis=0, tiled=True),
    )


def col_totals(arrays):
    return (
        lax.psum_scatter(
            arrays[0].astype(jnp.bfloat16), "col", scatter_dimension=0, tiled=True
        ).astype(jnp.float32),
        lax.psum_scatter(
            arrays[1].astype(jnp.bfloat16), "col", scatter_dimension=0, tiled=True
        ).astype(jnp.float32),
    )


def row_panels(arrays):
    return (
        lax.all_gather(arrays[0], "row", axis=0, tiled=True),
        lax.all_gather(arrays[1], "row", axis=0, tiled=True),
    )


def row_totals(arrays):
    return jax.tree.map(
        lambda part: part.astype(jnp.float32),
        lax.psum_scatter(for_sending(arrays), "row", scatter_dimension=0, tiled=True),
    )


def shards(
    out_first, out_second, grad_first, grad_second, w_query, w_key, w_value, w_out, w_up, w_down
):
    score_scale = 1.0 / math.sqrt(HEAD)
    inputs_all, grads_all = col_panels(
        (out_first.astype(jnp.bfloat16), grad_second.astype(jnp.bfloat16))
    )
    pre_term = jnp.dot(inputs_all, w_up, preferred_element_type=jnp.float32)
    back_term = times_trans(grads_all, w_down)
    pre_sum, back_sum = row_totals((pre_term, back_term))
    act_value, change = tanh_gelu(pre_sum)
    hidden_all, slope_all = row_panels(
        (act_value.astype(jnp.bfloat16), (back_sum * change).astype(jnp.bfloat16))
    )
    grad_down = trans_times(hidden_all, grads_all).astype(jnp.bfloat16)
    grad_up = trans_times(inputs_all, slope_all).astype(jnp.bfloat16)
    ffn_out, ffn_back = col_totals(
        (
            jnp.dot(hidden_all, w_down, preferred_element_type=jnp.float32),
            times_trans(slope_all, w_up),
        )
    )
    input_second = out_second - ffn_out
    grad_input_first = grad_first + ffn_back
    mid_all, carry_all = col_panels(
        (input_second.astype(jnp.bfloat16), grad_input_first.astype(jnp.bfloat16))
    )
    queries, key_rows, value_rows, out_grad = row_totals(
        (
            jnp.dot(mid_all, w_query, preferred_element_type=jnp.float32),
            jnp.dot(mid_all, w_key, preferred_element_type=jnp.float32),
            jnp.dot(mid_all, w_value, preferred_element_type=jnp.float32),
            times_trans(carry_all, w_out),
        )
    )
    queries = queries.astype(jnp.bfloat16)
    out_grad = out_grad.astype(jnp.bfloat16)
    keys_all, values_all = row_panels(
        (key_rows.astype(jnp.bfloat16), value_rows.astype(jnp.bfloat16))
    )
    rows_here = queries.shape[0]
    head_cols = queries.shape[1]
    heads_here = head_cols // HEAD
    key_count = keys_all.shape[0]
    query_heads = queries.reshape(rows_here, heads_here, HEAD)
    grad_heads = out_grad.reshape(rows_here, heads_here, HEAD)
    key_heads = keys_all.reshape(key_count, heads_here, HEAD)
    value_heads = values_all.reshape(key_count, heads_here, HEAD)
    query_pos = lax.axis_index("row") * rows_here + lax.iota(jnp.int32, rows_here)
    key_pos = lax.iota(jnp.int32, key_count)
    allowed = key_pos[None, :] <= query_pos[:, None]
    scores = (
        jnp.einsum("qhd,khd->hqk", query_heads, key_heads, preferred_element_type=jnp.float32)
        * score_scale
    )
    scores = jnp.where(allowed[None], scores, -1e30)
    peak = jnp.max(scores, axis=-1, keepdims=True)
    weights = jnp.exp(scores - peak)
    probs = weights / jnp.sum(weights, axis=-1, keepdims=True)
    probs_b = probs.astype(jnp.bfloat16)
    attended = (
        jnp.einsum("hqk,khd->qhd", probs_b, value_heads, preferred_element_type=jnp.float32)
        .astype(jnp.bfloat16)
        .reshape(rows_here, head_cols)
    )
    dprob = jnp.einsum("qhd,khd->hqk", grad_heads, value_heads, preferred_element_type=jnp.float32)
    delta = jnp.sum(probs * dprob, axis=-1, keepdims=True)
    dscore_b = (probs * (dprob - delta)).astype(jnp.bfloat16)
    grad_queries = (
        (
            score_scale
            * jnp.einsum("hqk,khd->qhd", dscore_b, key_heads, preferred_element_type=jnp.float32)
        )
        .astype(jnp.bfloat16)
        .reshape(rows_here, head_cols)
    )
    key_term = (
        score_scale
        * jnp.einsum("hqk,qhd->khd", dscore_b, query_heads, preferred_element_type=jnp.float32)
    ).reshape(key_count, head_cols)
    value_term = jnp.einsum(
        "hqk,qhd->khd", probs_b, grad_heads, preferred_element_type=jnp.float32
    ).reshape(key_count, head_cols)
    key_sum, value_sum = (
        lax.psum(key_term.astype(jnp.bfloat16), "row").astype(jnp.float32),
        lax.psum(value_term.astype(jnp.bfloat16), "row").astype(jnp.float32),
    )
    attended_all, gradq_all = row_panels((attended, grad_queries))
    gradk_all = key_sum.astype(jnp.bfloat16)
    gradv_all = value_sum.astype(jnp.bfloat16)
    grad_mid = (
        times_trans(gradq_all, w_query)
        + times_trans(gradk_all, w_key)
        + times_trans(gradv_all, w_value)
    )
    attn_out, back_mid = col_totals(
        (jnp.dot(attended_all, w_out, preferred_element_type=jnp.float32), grad_mid)
    )
    input_first = out_first - attn_out
    grad_input_second = grad_second + back_mid
    return (input_first, input_second, grad_input_first, grad_input_second, grad_up, grad_down)


def solution(mesh):
    in_specs = (
        P(("grp", "col"), "row"),
        P(("grp", "col"), "row"),
        P(("grp", "col"), "row"),
        P(("grp", "col"), "row"),
        P("row", "col"),
        P("row", "col"),
        P("row", "col"),
        P("col", "row"),
        P("row", "col"),
        P("col", "row"),
    )
    out_specs = (
        P(("grp", "col"), "row"),
        P(("grp", "col"), "row"),
        P(("grp", "col"), "row"),
        P(("grp", "col"), "row"),
        P(("grp", "row"), "col"),
        P(("grp", "col"), "row"),
    )
    return jax.shard_map(shards, mesh=mesh, in_specs=in_specs, out_specs=out_specs, check_vma=False)
```

profile of v0, /device:TPU:0, one launch (start us, length us, event | category | flops | bytes accessed | tf_op | source)
XLA Modules:
  0.0 610.8 jit_solution(4323098131918377079)
XLA Ops:
  8.2 10.0 %all_gather.30 = bf16[256,1536]{1,0:T(8,128)(2,1)S(1)} all-gather(bf16[64,1536]{1,0:T(8,128)(2,1)S(1)} %convert_element_type.123), channel_id=1, replica_groups=mesh['grp'=2,'row'=4,'col'=4] {'col'}, dimensions={0}, use_global_device_ids=true | all-gather | bytes 983040 | tf_op jit(solution)/shard_map/all_gather | solution.py:39
  19.2 13.5 %convolution_convert_fusion.3 = bf16[256,6144]{1,0:T(8,128)(2,1)} fusion(bf16[256,1536]{1,0:T(8,128)(2,1)S(1)} %all_gather.30, bf16[1536,6144]{1,0:T(8,128)(2,1)} %param.18), kind=kOutput, calls=%fused_computation.5 | convolution fusion | flops 4833411072 | bytes 22806528 | tf_op jit(solution)/shard_map/dot_general | solution.py:76
  33.7 8.7 %all_gather.36 = bf16[256,1536]{1,0:T(8,128)(2,1)S(1)} all-gather(bf16[64,1536]{1,0:T(8,128)(2,1)S(1)} %convert_element_type.138), channel_id=1, replica_groups=mesh['grp'=2,'row'=4,'col'=4] {'col'}, dimensions={0}, use_global_device_ids=true | all-gather | bytes 983040 | tf_op jit(solution)/shard_map/all_gather | solution.py:40
  43.3 10.3 %convolution_convert_fusion.2 = bf16[256,6144]{1,0:T(8,128)(2,1)} fusion(bf16[256,1536]{1,0:T(8,128)(2,1)S(1)} %all_gather.36, bf16[6144,1536]{1,0:T(8,128)(2,1)} %param.19), kind=kOutput, calls=%fused_computation.4 | convolution fusion | flops 4833411072 | bytes 22806528 | tf_op jit(solution)/shard_map/dot_general | solution.py:26
  53.7 40.3 %reduce-scatter.11.cloned.1.call-done = bf16[64,6144]{1,0:T(8,128)(2,1)} async-done(((bf16[256,6144]{1,0:T(8,128)(2,1)}), bf16[64,6144]{1,0:T(8,128)(2,1)}) %reduce-scatter.11.cloned.1.call-update) | async-done | bytes 786448 | tf_op jit(solution)/shard_map/reduce_scatter | solution.py:65
  94.0 63.2 %reduce-scatter.23.cloned.1.call-done = bf16[64,6144]{1,0:T(8,128)(2,1)} async-done(((bf16[256,6144]{1,0:T(8,128)(2,1)}), bf16[64,6144]{1,0:T(8,128)(2,1)}) %reduce-scatter.23.cloned.1.call-update) | async-done | bytes 786448 | tf_op jit(solution)/shard_map/reduce_scatter | solution.py:65
  161.5 63.1 %all-gather.3.cloned.1.call-done = bf16[256,6144]{1,0:T(8,128)(2,1)} async-done(((bf16[64,6144]{1,0:T(8,128)(2,1)}), bf16[256,6144]{1,0:T(8,128)(2,1)}) %all-gather.3.cloned.1.call-update) | async-done | bytes 3145744 | tf_op jit(solution)/shard_map/all_gather | solution.py:57
  224.6 10.7 %convolution_convert_fusion.5 = bf16[256,1536]{1,0:T(8,128)(2,1)} fusion(bf16[256,6144]{1,0:T(8,128)(2,1)} %all-gather.3.cloned.1.call-done, bf16[6144,1536]{1,0:T(8,128)(2,1)} %param.19), kind=kOutput, calls=%fused_computation.16 | convolution fusion | flops 4832231424 | bytes 22806528 | tf_op jit(solution)/shard_map/dot_general | solution.py:87
  235.3 53.4 %all-gather.5.cloned.1.call-done = bf16[256,6144]{1,0:T(8,128)(2,1)} async-done(((bf16[64,6144]{1,0:T(8,128)(2,1)}), bf16[256,6144]{1,0:T(8,128)(2,1)}) %all-gather.5.cloned.1.call-update) | async-done | bytes 3145744 | tf_op jit(solution)/shard_map/all_gather | solution.py:58
  288.8 10.8 %convolution_convert_fusion.4 = bf16[256,1536]{1,0:T(8,128)(2,1)} fusion(bf16[256,6144]{1,0:T(8,128)(2,1)} %all-gather.5.cloned.1.call-done, bf16[1536,6144]{1,0:T(8,128)(2,1)} %param.18), kind=kOutput, calls=%fused_computation.15 | convolution fusion | flops 4832231424 | bytes 22806528 | tf_op jit(solution)/shard_map/dot_general | solution.py:26
  299.6 14.0 %reduce-scatter.13.cloned.1.call-done = bf16[64,1536]{1,0:T(8,128)(2,1)} async-done(((bf16[256,1536]{1,0:T(8,128)(2,1)}), bf16[64,1536]{1,0:T(8,128)(2,1)}) %reduce-scatter.13.cloned.1.call-update) | async-done | bytes 196624 | tf_op jit(solution)/shard_map/reduce_scatter | solution.py:46
  315.4 8.4 %all_gather.32 = bf16[256,1536]{1,0:T(8,128)(2,1)S(1)} all-gather(bf16[64,1536]{1,0:T(8,128)(2,1)S(1)} %get-tuple-element.22), channel_id=1, replica_groups=mesh['grp'=2,'row'=4,'col'=4] {'col'}, dimensions={0}, use_global_device_ids=true | all-gather | bytes 983040 | tf_op jit(solution)/shard_map/all_gather | solution.py:39
  341.2 8.2 %all_gather.38 = bf16[256,1536]{1,0:T(8,128)(2,1)S(1)} all-gather(bf16[64,1536]{1,0:T(8,128)(2,1)S(1)} %get-tuple-element.20), channel_id=1, replica_groups=mesh['grp'=2,'row'=4,'col'=4] {'col'}, dimensions={0}, use_global_device_ids=true | all-gather | bytes 983040 | tf_op jit(solution)/shard_map/all_gather | solution.py:40
  354.3 11.4 %reduce-scatter.19.cloned.1.call-done = bf16[64,1536]{1,0:T(8,128)(2,1)} async-done(((bf16[256,1536]{1,0:T(8,128)(2,1)}), bf16[64,1536]{1,0:T(8,128)(2,1)}) %reduce-scatter.19.cloned.1.call-update) | async-done | bytes 196624 | tf_op jit(solution)/shard_map/reduce_scatter | solution.py:65
  365.7 23.1 %all_gather.34 = bf16[256,1536]{1,0:T(8,128)(2,1)S(1)} all-gather(bf16[64,1536]{1,0:T(8,128)(2,1)} %reduce-scatter.19.cloned.1.call-done), channel_id=1, replica_groups=mesh['grp'=2,'row'=4,'col'=4] {'row'}, dimensions={0}, use_global_device_ids=true | all-gather | bytes 983040 | tf_op jit(solution)/shard_map/all_gather | solution.py:57
  389.0 7.2 %reduce-scatter.15.cloned.1.call-done = bf16[64,1536]{1,0:T(8,128)(2,1)} async-done(((bf16[256,1536]{1,0:T(8,128)(2,1)}), bf16[64,1536]{1,0:T(8,128)(2,1)}) %reduce-scatter.15.cloned.1.call-update) | async-done | bytes 196624 | tf_op jit(solution)/shard_map/reduce_scatter | solution.py:65
  396.2 24.5 %all_gather.33 = bf16[256,1536]{1,0:T(8,128)(2,1)S(1)} all-gather(bf16[64,1536]{1,0:T(8,128)(2,1)} %reduce-scatter.15.cloned.1.call-done), channel_id=1, replica_groups=mesh['grp'=2,'row'=4,'col'=4] {'row'}, dimensions={0}, use_global_device_ids=true | all-gather | bytes 983040 | tf_op jit(solution)/shard_map/all_gather | solution.py:58
  430.8 22.2 %reduce-scatter.27.cloned.1.call-done = bf16[64,1536]{1,0:T(8,128)(2,1)} async-done(((bf16[256,1536]{1,0:T(8,128)(2,1)}), bf16[64,1536]{1,0:T(8,128)(2,1)}) %reduce-scatter.27.cloned.1.call-update) | async-done | bytes 196624 | tf_op jit(solution)/shard_map/reduce_scatter | solution.py:65
  462.2 27.4 %all_gather.35 = bf16[256,1536]{1,0:T(8,128)(2,1)S(1)} all-gather(bf16[64,1536]{1,0:T(8,128)(2,1)S(1)} %bitcast.92), channel_id=1, replica_groups=mesh['grp'=2,'row'=4,'col'=4] {'row'}, dimensions={0}, use_global_device_ids=true | all-gather | bytes 983040 | tf_op jit(solution)/shard_map/all_gather | solution.py:57
  494.4 23.6 %all_gather.39 = bf16[256,1536]{1,0:T(8,128)(2,1)S(1)} all-gather(bf16[64,1536]{1,0:T(8,128)(2,1)S(1)} %bitcast.91), channel_id=1, replica_groups=mesh['grp'=2,'row'=4,'col'=4] {'row'}, dimensions={0}, use_global_device_ids=true | all-gather | bytes 983040 | tf_op jit(solution)/shard_map/all_gather | solution.py:58
  521.8 23.7 %all-reduce.3.cloned.1.call-done = (bf16[256,1536]{0,1:T(8,128)(2,1)}, bf16[256,1536]{0,1:T(8,128)(2,1)}) async-done(((bf16[256,1536]{0,1:T(8,128)(2,1)}, bf16[256,1536]{0,1:T(8,128)(2,1)}), (bf16[256,1536]{0,1:T(8,128)(2,1)}, bf16[256,1536]{0,1:T(8,128)(2,1)})) %all-reduce.3.cloned.1.call-update) | async-done | bytes 1572880 | tf_op jit(solution)/shard_map/psum | solution.py:153
  554.5 10.7 %fusion.1 = bf16[1536,6144]{0,1:T(8,128)(2,1)} fusion(bf16[256,6144]{1,0:T(8,128)(2,1)S(1)} %copy-done.1, bf16[256,1536]{1,0:T(8,128)(2,1)} %copy-done.2), kind=kOutput, calls=%fused_computation.3 | convolution fusion | flops 4841275392 | bytes 22806528 | tf_op jit(solution)/shard_map/dot_general | solution.py:32
  565.2 24.8 %copy.37 = bf16[1536,6144]{1,0:T(8,128)(2,1)} copy(bf16[1536,6144]{0,1:T(8,128)(2,1)} %fusion.1) | data formatting | bytes 37748736
  590.0 10.7 %convolution_convert_fusion = bf16[6144,1536]{1,0:T(8,128)(2,1)} fusion(bf16[256,6144]{1,0:T(8,128)(2,1)S(1)} %copy-done, bf16[256,1536]{1,0:T(8,128)(2,1)} %copy-done.3), kind=kOutput, calls=%fused_computation.1 | convolution fusion | flops 4841275392 | bytes 22806528 | tf_op jit(solution)/shard_map/dot_general | solution.py:32
  (77 shorter events, 72.8 us)
Async XLA Ops:
  7.2 86.8 %reduce-scatter.11.cloned.1.call-start = ((), (), s32[]{:S(2)}) async-start(), calls=%async_computation.10 | async-start | bytes 3932160 | tf_op jit(solution)/shard_map/reduce_scatter | solution.py:65
  18.3 0.9 copy-start.2
  32.7 1.0 copy-start.5
  32.7 124.5 %reduce-scatter.23.cloned.1.call-start = ((), (), s32[]{:S(2)}) async-start(), calls=%async_computation.17 | async-start | bytes 3932160 | tf_op jit(solution)/shard_map/reduce_scatter | solution.py:65
  42.4 0.9 copy-start.3
  53.6 170.9 %all-gather.3.cloned.1.call-start = ((), (), s32[]{:S(2)}) async-start(), calls=%async_computation.11 | async-start | bytes 3932160 | tf_op jit(solution)/shard_map/all_gather | solution.py:57
  160.9 127.9 %all-gather.5.cloned.1.call-start = ((), (), s32[]{:S(2)}) async-start(), calls=%async_computation.18 | async-start | bytes 3932160 | tf_op jit(solution)/shard_map/all_gather | solution.py:58
  161.5 152.2 %reduce-scatter.13.cloned.1.call-start = ((), (), s32[]{:S(2)}) async-start(), calls=%async_computation.12 | async-start | bytes 983040 | tf_op jit(solution)/shard_map/reduce_scatter | solution.py:46
  235.2 78.4 %copy-start.6 = (f32[64,1536]{1,0:T(8,128)S(1)}, f32[64,1536]{1,0:T(8,128)}, u32[]{:S(2)}) copy-start(f32[64,1536]{1,0:T(8,128)} %param.11) | copy-start | bytes 1179652
  235.3 104.2 %reduce-scatter.25.cloned.1.call-start = ((), (), s32[]{:S(2)}) async-start(), calls=%async_computation.19 | async-start | bytes 983040 | tf_op jit(solution)/shard_map/reduce_scatter | solution.py:49
  299.6 66.1 %reduce-scatter.19.cloned.1.call-start = ((), (), s32[]{:S(2)}) async-start(), calls=%async_computation.15 | async-start | bytes 983040 | tf_op jit(solution)/shard_map/reduce_scatter | solution.py:65
  328.4 67.8 %reduce-scatter.15.cloned.1.call-start = ((), (), s32[]{:S(2)}) async-start(), calls=%async_computation.13 | async-start | bytes 983040 | tf_op jit(solution)/shard_map/reduce_scatter | solution.py:65
  333.1 6.4 %copy-start.7 = (f32[64,1536]{1,0:T(8,128)S(1)}, f32[64,1536]{1,0:T(8,128)}, u32[]{:S(2)}) copy-start(f32[64,1536]{1,0:T(8,128)} %param.12) | copy-start | bytes 1179652
  333.1 94.4 %reduce-scatter.17.cloned.1.call-start = ((), (), s32[]{:S(2)}) async-start(), calls=%async_computation.14 | async-start | bytes 983040 | tf_op jit(solution)/shard_map/reduce_scatter | solution.py:65
  337.9 115.0 %reduce-scatter.27.cloned.1.call-start = ((), (), s32[]{:S(2)}) async-start(), calls=%async_computation.20 | async-start | bytes 983040 | tf_op jit(solution)/shard_map/reduce_scatter | solution.py:65
  354.2 191.3 %all-reduce.3.cloned.1.call-start = ((), (), s32[]{:S(2)}) async-start(), calls=%async_computation.22 | async-start | bytes 3145728 | tf_op jit(solution)/shard_map/psum | solution.py:153
  460.2 140.5 %reduce-scatter.21.cloned.1.call-start = ((), (), s32[]{:S(2)}) async-start(), calls=%async_computation.16 | async-start | bytes 983040 | tf_op jit(solution)/shard_map/reduce_scatter | solution.py:46
  494.3 108.1 %reduce-scatter.29.cloned.1.call-start = ((), (), s32[]{:S(2)}) async-start(), calls=%async_computation.21 | async-start | bytes 983040 | tf_op jit(solution)/shard_map/reduce_scatter | solution.py:49
  545.4 4.1 copy-start.8
  549.5 5.0 copy-start.1
  565.2 24.8 %copy-start = (bf16[256,6144]{1,0:T(8,128)(2,1)S(1)}, bf16[256,6144]{1,0:T(8,128)(2,1)}, u32[]{:S(2)}) copy-start(bf16[256,6144]{1,0:T(8,128)(2,1)} %all-gather.3.cloned.1.call-done) | copy-start | bytes 9437188
  590.0 10.7 %copy-start.4 = (f32[64,1536]{1,0:T(8,128)S(1)}, f32[64,1536]{1,0:T(8,128)}, u32[]{:S(2)}) copy-start(f32[64,1536]{1,0:T(8,128)} %param.10) | copy-start | bytes 1179652
Sparse Core Ops, SparseCore 0:
  32.8 61.1 reduce-scatter.10
  96.9 60.2 reduce-scatter.22
  161.0 63.5 all-gather.2
  226.6 62.1 all-gather.4
  291.7 21.8 reduce-scatter.12
  316.2 23.2 reduce-scatter.24
  342.4 23.2 reduce-scatter.18
  368.6 27.6 reduce-scatter.14
  398.6 28.9 reduce-scatter.16
  429.7 23.2 reduce-scatter.26
  460.3 85.0 all-reduce.2
  547.8 22.3 reduce-scatter.20
  572.9 23.2 reduce-scatter.28
where the time goes:
time: 612 us; the launch traced here: 611 us
  waiting for transfers between devices  307 us (50%)
  blocking collectives  134 us (22%)
  matrix products  113 us (18%)
  local copies, waits for them, and re-layouts  28.2 us (5%)
  other arithmetic  14.1 us (2%)
  between operations  14.1 us (2%)
    reduce_scatter x6, waiting for transfers between devices, row_totals(): lax.psum_scatter(for_sending(arrays), 'row', scatter_dimension=0, tiled=T...  151 us
    all_gather x1, waiting for transfers between devices, row_panels(): lax.all_gather(arrays[0], 'row', axis=0, tiled=True)  63.1 us
    all_gather x1, waiting for transfers between devices, row_panels(): lax.all_gather(arrays[1], 'row', axis=0, tiled=True)  53.4 us
    all_gather x2, blocking collectives, row_panels(): lax.all_gather(arrays[0], 'row', axis=0, tiled=True)  50.5 us
    all_gather x2, blocking collectives, row_panels(): lax.all_gather(arrays[1], 'row', axis=0, tiled=True)  48.1 us
    dot_general x6, matrix products, times_trans(): lax.dot_general(first_op, second_op, (((1,), (1,)), ((), ())), preferred_...  38.6 us
    unnamed x19, local copies, waits for them, and re-layouts  27.5 us
    psum x1, waiting for transfers between devices, shards(): lax.psum(key_term.astype(jnp.bfloat16), 'row').astype(jnp.float32)  23.7 us
  transfers between devices with their start and end apart: 13, of which 11 were waited for; matrix products, arithmetic and copies ran while one was open for 20% of the time, Pallas kernels for 0%

commit v1 on v0

--- a/solution.py
+++ b/solution.py
@@ -1,8 +1,11 @@
+import functools
 import math
 
 import jax
 import jax.numpy as jnp
 from jax import lax
+from jax.experimental import pallas as pl
+from jax.experimental.pallas import tpu as pltpu
 from jax.sharding import PartitionSpec as P
 
 HEAD = 128
@@ -65,42 +68,259 @@
         lax.psum_scatter(for_sending(arrays), "row", scatter_dimension=0, tiled=True),
     )
 
-
-def shards(
-    out_first, out_second, grad_first, grad_second, w_query, w_key, w_value, w_out, w_up, w_down
-):
+def chain_kernel(n, count, chunks, ds_of, middle, *refs):
+    ins, out = refs[:count], refs[count]
+    right_buf, left_buf = refs[count + 1 : count + 3]
+    sems = refs[count + 3 :]
+    me = lax.axis_index("row")
+    has_left, has_right = me > 0, me < n - 1
+
+    def copy(buf, kind, k, b, target):
+        rows, cols = ds_of(b, k)
+        part = buf.at[:, rows, cols]
+        return pltpu.make_async_remote_copy(
+            src_ref=part,
+            dst_ref=part,
+            send_sem=sems[2 * kind].at[k * n + b],
+            recv_sem=sems[2 * kind + 1].at[k * n + b],
+            device_id={"row": target},
+            device_id_type=pl.DeviceIdType.MESH,
+        )
+
+    def rs_right(k, b):
+        return copy(right_buf, 0, k, b, me + 1)
+
+    def rs_left(k, b):
+        return copy(left_buf, 1, k, b, me - 1)
+
+    def ag_right(k, b):
+        return copy(out, 2, k, b, me + 1)
+
+    def ag_left(k, b):
+        return copy(out, 3, k, b, me - 1)
+
+    barrier = pltpu.get_barrier_semaphore()
+
+    @pl.when(has_left)
+    def _():
+        pl.semaphore_signal(
+            barrier, inc=1, device_id={"row": me - 1}, device_id_type=pl.DeviceIdType.MESH
+        )
+
+    @pl.when(has_right)
+    def _():
+        pl.semaphore_signal(
+            barrier, inc=1, device_id={"row": me + 1}, device_id_type=pl.DeviceIdType.MESH
+        )
+
+    pl.semaphore_wait(barrier, has_left.astype(jnp.int32) + has_right.astype(jnp.int32))
+
+    def own_into(buf, k, b, add):
+        rows, cols = ds_of(b, k)
+
+        @pl.loop(0, rows.size // 16)
+        def _(r):
+            piece = pl.ds(pl.multiple_of(rows.start + r * 16, 16), 16)
+            for s in range(count):
+                val = ins[s][piece, cols]
+                if add:
+                    val = (val.astype(jnp.float32) + buf[s, piece, cols].astype(jnp.float32)).astype(
+                        jnp.bfloat16
+                    )
+                buf[s, piece, cols] = val
+
+    def hop(buf, make, k, b, has_source):
+        @pl.when(has_source)
+        def _():
+            make(k, b).wait_recv()
+            own_into(buf, k, b, True)
+
+        @pl.when(jnp.logical_not(has_source))
+        def _():
+            own_into(buf, k, b, False)
+
+        make(k, b).start()
+
+    def zero(buf, k):
+        rows, cols = ds_of(me, k)
+        buf[:, rows, cols] = jnp.zeros((count, rows.size, cols.size), jnp.bfloat16)
+
+    def reduce(k):
+        for j in range(n):
+
+            @pl.when(n - 1 - j > me)
+            def _():
+                hop(right_buf, rs_right, k, n - 1 - j, has_left)
+
+            @pl.when(j < me)
+            def _():
+                hop(left_buf, rs_left, k, j, has_right)
+
+        @pl.when(has_left)
+        def _():
+            rs_right(k, me).wait_recv()
+
+        @pl.when(jnp.logical_not(has_left))
+        def _():
+            zero(right_buf, k)
+
+        @pl.when(has_right)
+        def _():
+            rs_left(k, me).wait_recv()
+
+        @pl.when(jnp.logical_not(has_right))
+        def _():
+            zero(left_buf, k)
+
+        rows, cols = ds_of(me, k)
+        middle(ins, right_buf, left_buf, out, rows, cols)
+
+        @pl.when(has_right)
+        def _():
+            ag_right(k, me).start()
+
+        @pl.when(has_left)
+        def _():
+            ag_left(k, me).start()
+
+    def gather(k):
+        for d in range(1, n):
+
+            @pl.when(me - d >= 0)
+            def _():
+                ag_right(k, me - d).wait_recv()
+
+                @pl.when(has_right)
+                def _():
+                    ag_right(k, me - d).start()
+
+            @pl.when(me + d < n)
+            def _():
+                ag_left(k, me + d).wait_recv()
+
+                @pl.when(has_left)
+                def _():
+                    ag_left(k, me + d).start()
+
+    reduce(0)
+
+    @pl.loop(1, chunks)
+    def _(k):
+        reduce(k)
+        gather(k - 1)
+
+    gather(chunks - 1)
+
+    @pl.loop(0, chunks)
+    def _(k):
+        for b in range(n):
+
+            @pl.when(b > me)
+            def _():
+                rs_right(k, b).wait_send()
+
+            @pl.when(b < me)
+            def _():
+                rs_left(k, b).wait_send()
+
+            @pl.when(jnp.logical_and(b <= me, has_right))
+            def _():
+                ag_right(k, b).wait_send()
+
+            @pl.when(jnp.logical_and(b >= me, has_left))
+            def _():
+                ag_left(k, b).wait_send()
+
+
+def chain_exchange(n, arrays, chunks, ds_of, middle, collective_id):
+    count = len(arrays)
+    tokens, width = arrays[0].shape
+    full = (count, tokens, width)
+    return pl.pallas_call(
+        functools.partial(chain_kernel, n, count, chunks, ds_of, middle),
+        out_shape=jax.ShapeDtypeStruct(full, jnp.bfloat16),
+        in_specs=[pl.BlockSpec(memory_space=pltpu.VMEM)] * count,
+        out_specs=pl.BlockSpec(memory_space=pltpu.VMEM),
+        scratch_shapes=[pltpu.VMEM(full, jnp.bfloat16)] * 2
+        + [pltpu.SemaphoreType.DMA((chunks * n,))] * 8,
+        compiler_params=pltpu.CompilerParams(
+            collective_id=collective_id,
+            has_side_effects=True,
+            vmem_limit_bytes=min(60 << 20, (4 * count + 1) * tokens * width * 2 + (12 << 20)),
+        ),
+    )(*arrays)
+
+
+def ffn_middle(ins, right_buf, left_buf, out, rows, cols):
+    @pl.loop(0, rows.size // 16)
+    def _(r):
+        piece = pl.ds(pl.multiple_of(rows.start + r * 16, 16), 16)
+        pre_sum, back_sum = (
+            ins[s][piece, cols].astype(jnp.float32)
+            + right_buf[s, piece, cols].astype(jnp.float32)
+            + left_buf[s, piece, cols].astype(jnp.float32)
+            for s in range(2)
+        )
+        act_value, change = tanh_gelu(pre_sum)
+        out[0, piece, cols] = act_value.astype(jnp.bfloat16)
+        out[1, piece, cols] = (back_sum * change).astype(jnp.bfloat16)
+
+
+def attention_middle(ins, right_buf, left_buf, out, rows, cols):
+    queries, keys, values, out_grad = (
+        (
+            ins[s][rows, cols].astype(jnp.float32)
+            + right_buf[s, rows, cols].astype(jnp.float32)
+            + left_buf[s, rows, cols].astype(jnp.float32)
+        ).astype(jnp.bfloat16)
+        for s in range(4)
+    )
     score_scale = 1.0 / math.sqrt(HEAD)
-    inputs_all, grads_all = col_panels(
-        (out_first.astype(jnp.bfloat16), grad_second.astype(jnp.bfloat16))
-    )
-    pre_term = jnp.dot(inputs_all, w_up, preferred_element_type=jnp.float32)
-    back_term = times_trans(grads_all, w_down)
-    pre_sum, back_sum = row_totals((pre_term, back_term))
-    act_value, change = tanh_gelu(pre_sum)
-    hidden_all, slope_all = row_panels(
-        (act_value.astype(jnp.bfloat16), (back_sum * change).astype(jnp.bfloat16))
-    )
-    grad_down = trans_times(hidden_all, grads_all).astype(jnp.bfloat16)
-    grad_up = trans_times(inputs_all, slope_all).astype(jnp.bfloat16)
-    ffn_out, ffn_back = col_totals(
-        (
-            jnp.dot(hidden_all, w_down, preferred_element_type=jnp.float32),
-            times_trans(slope_all, w_up),
-        )
-    )
-    input_second = out_second - ffn_out
-    grad_input_first = grad_first + ffn_back
-    mid_all, carry_all = col_panels(
-        (input_second.astype(jnp.bfloat16), grad_input_first.astype(jnp.bfloat16))
-    )
-    queries, key_rows, value_rows, out_grad = row_totals(
-        (
-            jnp.dot(mid_all, w_query, preferred_element_type=jnp.float32),
-            jnp.dot(mid_all, w_key, preferred_element_type=jnp.float32),
-            jnp.dot(mid_all, w_value, preferred_element_type=jnp.float32),
-            times_trans(carry_all, w_out),
-        )
-    )
+    tokens = queries.shape[0]
+    scores = times_trans(queries, keys) * score_scale
+    query_pos = lax.broadcasted_iota(jnp.int32, (tokens, tokens), 0)
+    key_pos = lax.broadcasted_iota(jnp.int32, (tokens, tokens), 1)
+    scores = jnp.where(key_pos <= query_pos, scores, -1e30)
+    peak = jnp.max(scores, axis=-1, keepdims=True)
+    weights = jnp.exp(scores - peak)
+    probs = weights / jnp.sum(weights, axis=-1, keepdims=True)
+    probs_b = probs.astype(jnp.bfloat16)
+    out[0, rows, cols] = jnp.dot(probs_b, values, preferred_element_type=jnp.float32).astype(
+        jnp.bfloat16
+    )
+    dprob = times_trans(out_grad, values)
+    delta = jnp.sum(probs * dprob, axis=-1, keepdims=True)
+    dscore_b = (probs * (dprob - delta)).astype(jnp.bfloat16)
+    out[1, rows, cols] = (
+        score_scale * jnp.dot(dscore_b, keys, preferred_element_type=jnp.float32)
+    ).astype(jnp.bfloat16)
+    out[2, rows, cols] = (score_scale * trans_times(dscore_b, queries)).astype(jnp.bfloat16)
+    out[3, rows, cols] = trans_times(probs_b, out_grad).astype(jnp.bfloat16)
+
+
+def token_blocks(token_rows, chunk_width):
+    def ds_of(block, chunk):
+        return (
+            pl.ds(pl.multiple_of(block * token_rows, 16), token_rows),
+            pl.ds(pl.multiple_of(chunk * chunk_width, 128), chunk_width),
+        )
+
+    return ds_of
+
+
+def head_blocks(tokens, heads):
+    def ds_of(block, chunk):
+        return (
+            pl.ds(0, tokens),
+            pl.ds(pl.multiple_of((block * heads + chunk) * HEAD, HEAD), HEAD),
+        )
+
+    return ds_of
+
+
+def attention_by_tokens(projections):
+    score_scale = 1.0 / math.sqrt(HEAD)
+    queries, key_rows, value_rows, out_grad = row_totals(projections)
     queries = queries.astype(jnp.bfloat16)
     out_grad = out_grad.astype(jnp.bfloat16)
     keys_all, values_all = row_panels(
@@ -156,6 +376,63 @@
     attended_all, gradq_all = row_panels((attended, grad_queries))
     gradk_all = key_sum.astype(jnp.bfloat16)
     gradv_all = value_sum.astype(jnp.bfloat16)
+    return attended_all, gradq_all, gradk_all, gradv_all
+
+
+def shards(
+    out_first, out_second, grad_first, grad_second, w_query, w_key, w_value, w_out, w_up, w_down
+):
+    inputs_all, grads_all = col_panels(
+        (out_first.astype(jnp.bfloat16), grad_second.astype(jnp.bfloat16))
+    )
+    pre_term = jnp.dot(inputs_all, w_up, preferred_element_type=jnp.float32)
+    back_term = times_trans(grads_all, w_down)
+    n_row = lax.axis_size("row")
+    pre_term, back_term = for_sending((pre_term, back_term))
+    token_rows, hidden_width = pre_term.shape[0] // n_row, pre_term.shape[1]
+    ffn_chunks = max(c for c in (1, 2, 4, 8) if hidden_width % (c * 128) == 0)
+    hidden_slope = chain_exchange(
+        n_row,
+        (pre_term, back_term),
+        ffn_chunks,
+        token_blocks(token_rows, hidden_width // ffn_chunks),
+        ffn_middle,
+        1,
+    )
+    hidden_all, slope_all = hidden_slope[0], hidden_slope[1]
+    grad_down = trans_times(hidden_all, grads_all).astype(jnp.bfloat16)
+    grad_up = trans_times(inputs_all, slope_all).astype(jnp.bfloat16)
+    ffn_out, ffn_back = col_totals(
+        (
+            jnp.dot(hidden_all, w_down, preferred_element_type=jnp.float32),
+            times_trans(slope_all, w_up),
+        )
+    )
+    input_second = out_second - ffn_out
+    grad_input_first = grad_first + ffn_back
+    mid_all, carry_all = col_panels(
+        (input_second.astype(jnp.bfloat16), grad_input_first.astype(jnp.bfloat16))
+    )
+    projections = (
+        jnp.dot(mid_all, w_query, preferred_element_type=jnp.float32),
+        jnp.dot(mid_all, w_key, preferred_element_type=jnp.float32),
+        jnp.dot(mid_all, w_value, preferred_element_type=jnp.float32),
+        times_trans(carry_all, w_out),
+    )
+    heads_local = w_query.shape[1] // HEAD
+    if heads_local % n_row == 0:
+        share = heads_local // n_row
+        results = chain_exchange(
+            n_row,
+            for_sending(projections),
+            share,
+            head_blocks(projections[0].shape[0], share),
+            attention_middle,
+            2,
+        )
+        attended_all, gradq_all, gradk_all, gradv_all = (results[s] for s in range(4))
+    else:
+        attended_all, gradq_all, gradk_all, gradv_all = attention_by_tokens(projections)
     grad_mid = (
         times_trans(gradq_all, w_query)
         + times_trans(gradk_all, w_key)

time: 612 us -> 601 us (0.982)
  Pallas kernels: 0 us -> 402 us
  waiting for transfers between devices: 307 us -> 18.2 us
  blocking collectives: 134 us -> 35.6 us
  matrix products: 113 us -> 93.5 us
    pallas_call x0 -> x2, Pallas kernels: none -> 402 us  [chain_exchange(): pl.pallas_call(functools.partial(chain_kernel, n, count, chunks, ds_of, m...]
    reduce_scatter x6 -> x0, waiting for transfers between devices: 151 us -> none  [row_totals(): lax.psum_scatter(for_sending(arrays), 'row', scatter_dimension=0, tiled=T...]
    all_gather x2 -> x0, waiting for transfers between devices: 116 us -> none  [the longest x1 63.1 us: row_panels(): lax.all_gather(arrays[0], 'row', axis=0, tiled=True)]
    all_gather x4 -> x0, blocking collectives: 98.6 us -> none  [the longest x2 50.5 us: row_panels(): lax.all_gather(arrays[0], 'row', axis=0, tiled=True)]
    psum x1 -> x0, waiting for transfers between devices: 23.7 us -> none  [shards(): lax.psum(key_term.astype(jnp.bfloat16), 'row').astype(jnp.float32)]
    dot_general x6 -> x0, matrix products: 9.89 us -> none  [the longest x1 3.41 us: shards(): jnp.einsum('hqk,qhd->khd', probs_b, grad_heads, preferred_element_type=jn...]
    unnamed x19 -> x35, local copies, waits for them, and re-layouts: 27.5 us -> 27.5 us
  transfers between devices with their start and end apart: 13 -> 4, of which waited for: 11 -> 2; matrix products, arithmetic and copies ran while one was open for 20% -> 14% of each run, Pallas kernels for 0% -> 0%
where the time goes in v1:
time: 601 us; the launch traced here: 600 us
  Pallas kernels  402 us (67%)
  matrix products  93.5 us (16%)
  blocking collectives  35.6 us (6%)
  local copies, waits for them, and re-layouts  27.5 us (5%)
  waiting for transfers between devices  18.2 us (3%)
  between operations  13.9 us (2%)
  other arithmetic  9.15 us (2%)
    pallas_call x2, Pallas kernels, chain_exchange(): pl.pallas_call(functools.partial(chain_kernel, n, count, chunks, ds_of, m...  402 us
    dot_general x6, matrix products, times_trans(): lax.dot_general(first_op, second_op, (((1,), (1,)), ((), ())), preferred_...  34.2 us
    unnamed x35, local copies, waits for them, and re-layouts  27.5 us
    dot_general x2, matrix products, trans_times(): lax.dot_general(first_op, second_op, (((0,), (0,)), ((), ())), preferred_...  22.6 us
    all_gather x2, blocking collectives, col_panels(): lax.all_gather(arrays[0], 'col', axis=0, tiled=True)  18.6 us
    all_gather x2, blocking collectives, col_panels(): lax.all_gather(arrays[1], 'col', axis=0, tiled=True)  17 us
    dot_general x1, matrix products, shards(): pre_term = jnp.dot(inputs_all, w_up, preferred_element_type=jnp.float32)  12.6 us
  transfers between devices with their start and end apart: 4, of which 2 were waited for; matrix products, arithmetic and copies ran while one was open for 14% of the time, Pallas kernels for 0%

profile of v1, /device:TPU:0, one launch (start us, length us, event | category | flops | bytes accessed | tf_op | source)
XLA Modules:
  0.0 600.4 jit_solution(17575274329556349057)
XLA Ops:
  8.2 10.0 %all_gather.12 = bf16[256,1536]{1,0:T(8,128)(2,1)S(1)} all-gather(bf16[64,1536]{1,0:T(8,128)(2,1)S(1)} %convert_element_type.63), channel_id=1, replica_groups=mesh['grp'=2,'row'=4,'col'=4] {'col'}, dimensions={0}, use_global_device_ids=true | all-gather | bytes 983040 | tf_op jit(solution)/shard_map/all_gather | solution.py:42
  19.6 8.7 %all_gather.13 = bf16[256,1536]{1,0:T(8,128)(2,1)S(1)} all-gather(bf16[64,1536]{1,0:T(8,128)(2,1)S(1)} %convert_element_type.65), channel_id=1, replica_groups=mesh['grp'=2,'row'=4,'col'=4] {'col'}, dimensions={0}, use_global_device_ids=true | all-gather | bytes 983040 | tf_op jit(solution)/shard_map/all_gather | solution.py:43
  28.3 12.6 %convolution_convert_fusion.3.refs_0_ = bf16[256,6144]{1,0:T(8,128)(2,1)S(1)} fusion(bf16[256,1536]{1,0:T(8,128)(2,1)S(1)} %all_gather.12, bf16[1536,6144]{1,0:T(8,128)(2,1)} %param.18), kind=kOutput, calls=%fused_computation.4 | convolution fusion | flops 4833411072 | bytes 22806528 | tf_op jit(solution)/shard_map/dot_general | solution.py:388
  40.9 9.1 %convolution_convert_fusion.2.refs_1_ = bf16[256,6144]{1,0:T(8,128)(2,1)S(1)} fusion(bf16[256,1536]{1,0:T(8,128)(2,1)S(1)} %all_gather.13, bf16[6144,1536]{1,0:T(8,128)(2,1)} %param.19), kind=kOutput, calls=%fused_computation.3 | convolution fusion | flops 4833411072 | bytes 22806528 | tf_op jit(solution)/shard_map/dot_general | solution.py:29
  50.1 269.2 %shard_map.145 = bf16[2,256,6144]{2,1,0:T(8,128)(2,1)S(1)} custom-call(bf16[256,6144]{1,0:T(8,128)(2,1)S(1)} %convolution_convert_fusion.3.refs_0_, bf16[256,6144]{1,0:T(8,128)(2,1)S(1)} %convolution_convert_fusion.2.refs_1_), custom_call_target="tpu_custom_call" | custom-call | tf_op jit(solution)/shard_map/pallas_call | solution.py:239
  319.4 2.6 copy-done
  322.0 9.9 %fusion.11 = bf16[256,1536]{1,0:T(8,128)(2,1)} fusion(bf16[6144,1536]{1,0:T(8,128)(2,1)} %param.19, bf16[2,256,6144]{2,1,0:T(8,128)(2,1)S(1)} %shard_map.145), kind=kOutput, calls=%fused_computation.17 | convolution fusion | flops 4832231424 | bytes 22806528 | tf_op jit(solution)/shard_map/dot_general | solution.py:407
  332.0 11.1 %fusion.14 = bf16[256,1536]{1,0:T(8,128)(2,1)} fusion(bf16[1536,6144]{1,0:T(8,128)(2,1)} %param.18, bf16[2,256,6144]{2,1,0:T(8,128)(2,1)} %copy-done), kind=kOutput, calls=%fused_computation.18 | convolution fusion | flops 4832231424 | bytes 22806528 | tf_op jit(solution)/shard_map/dot_general | solution.py:29
  343.2 11.8 %reduce-scatter.5.cloned.1.call-done = bf16[64,1536]{1,0:T(8,128)(2,1)} async-done(((bf16[256,1536]{1,0:T(8,128)(2,1)}), bf16[64,1536]{1,0:T(8,128)(2,1)}) %reduce-scatter.5.cloned.1.call-update) | async-done | bytes 196624 | tf_op jit(solution)/shard_map/reduce_scatter | solution.py:49
  356.7 8.5 %all_gather.14 = bf16[256,1536]{1,0:T(8,128)(2,1)S(1)} all-gather(bf16[64,1536]{1,0:T(8,128)(2,1)S(1)} %get-tuple-element.14), channel_id=1, replica_groups=mesh['grp'=2,'row'=4,'col'=4] {'col'}, dimensions={0}, use_global_device_ids=true | all-gather | bytes 983040 | tf_op jit(solution)/shard_map/all_gather | solution.py:42
  365.2 4.8 convolution_convert_fusion.8.refs_0_
  370.1 2.3 convolution_convert_fusion.7.refs_1_
  372.4 2.3 convolution_convert_fusion.6.refs_2_
  374.7 6.3 %reduce-scatter.7.cloned.1.call-done = bf16[64,1536]{1,0:T(8,128)(2,1)} async-done(((bf16[256,1536]{1,0:T(8,128)(2,1)}), bf16[64,1536]{1,0:T(8,128)(2,1)}) %reduce-scatter.7.cloned.1.call-update) | async-done | bytes 196624 | tf_op jit(solution)/shard_map/reduce_scatter | solution.py:52
  382.7 8.3 %all_gather.15 = bf16[256,1536]{1,0:T(8,128)(2,1)S(1)} all-gather(bf16[64,1536]{1,0:T(8,128)(2,1)S(1)} %get-tuple-element.12), channel_id=1, replica_groups=mesh['grp'=2,'row'=4,'col'=4] {'col'}, dimensions={0}, use_global_device_ids=true | all-gather | bytes 983040 | tf_op jit(solution)/shard_map/all_gather | solution.py:43
  391.1 3.7 convolution_convert_fusion.5.refs_3_
  394.8 132.8 %shard_map.146 = bf16[4,256,1536]{2,1,0:T(8,128)(2,1)S(1)} custom-call(bf16[256,1536]{1,0:T(8,128)(2,1)S(1)} %copy-done.1, bf16[256,1536]{1,0:T(8,128)(2,1)S(1)} %copy-done.2, bf16[256,1536]{1,0:T(8,128)(2,1)S(1)} %copy-done.3, bf16[256,1536]{1,0:T(8,128)(2,1)S(1)} %convolution_convert_fusion.5.refs_3_), custom_call_target="tpu_custom_call" | custom-call | tf_op jit(solution)/shard_map/pallas_call | solution.py:239
  527.7 4.7 convolution_convert_fusion.4
  532.6 3.9 fusion.20
  536.6 4.0 convolution_add_fusion.1
  540.6 2.4 fusion.17
  543.0 11.1 %fusion = bf16[1536,6144]{0,1:T(8,128)(2,1)} fusion(bf16[256,1536]{1,0:T(8,128)(2,1)} %copy-done.6, bf16[2,256,6144]{2,1,0:T(8,128)(2,1)} %copy-done), kind=kOutput, calls=%fused_computation.2 | convolution fusion | flops 4841275392 | bytes 22806528 | tf_op jit(solution)/shard_map/dot_general | solution.py:35
  554.1 24.7 %copy.16 = bf16[1536,6144]{1,0:T(8,128)(2,1)} copy(bf16[1536,6144]{0,1:T(8,128)(2,1)} %fusion) | data formatting | bytes 37748736
  578.9 11.5 %convolution_convert_fusion = bf16[6144,1536]{1,0:T(8,128)(2,1)} fusion(bf16[256,1536]{1,0:T(8,128)(2,1)S(1)} %copy-done.5, bf16[2,256,6144]{2,1,0:T(8,128)(2,1)} %copy-done), kind=kOutput, calls=%fused_computation | convolution fusion | flops 4841275392 | bytes 22806528 | tf_op jit(solution)/shard_map/dot_general | solution.py:35
  (52 shorter events, 9.7 us)
Async XLA Ops:
  7.2 347.8 %reduce-scatter.5.cloned.1.call-start = ((), (), s32[]{:S(2)}) async-start(), calls=%async_computation.4 | async-start | bytes 983040 | tf_op jit(solution)/shard_map/reduce_scatter | solution.py:49
  18.3 10.0 %copy-start.6 = (bf16[256,1536]{1,0:T(8,128)(2,1)}, bf16[256,1536]{1,0:T(8,128)(2,1)S(1)}, u32[]{:S(2)}) copy-start(bf16[256,1536]{1,0:T(8,128)(2,1)S(1)} %all_gather.12) | copy-start | bytes 2359300
  28.3 12.7 %copy-start.4 = (bf16[256,1536]{1,0:T(8,128)(2,1)}, bf16[256,1536]{1,0:T(8,128)(2,1)S(1)}, u32[]{:S(2)}) copy-start(bf16[256,1536]{1,0:T(8,128)(2,1)S(1)} %all_gather.13) | copy-start | bytes 2359300
  319.4 2.7 copy-start
  332.0 23.0 %copy-start.9 = (f32[64,1536]{1,0:T(8,128)S(1)}, f32[64,1536]{1,0:T(8,128)}, u32[]{:S(2)}) copy-start(f32[64,1536]{1,0:T(8,128)} %param.11) | copy-start | bytes 1179652
  332.0 49.0 %reduce-scatter.7.cloned.1.call-start = ((), (), s32[]{:S(2)}) async-start(), calls=%async_computation.5 | async-start | bytes 983040 | tf_op jit(solution)/shard_map/reduce_scatter | solution.py:52
  343.1 247.3 %reduce-scatter.9.cloned.1.call-start = ((), (), s32[]{:S(2)}) async-start(), calls=%async_computation.6 | async-start | bytes 983040 | tf_op jit(solution)/shard_map/reduce_scatter | solution.py:49
  356.7 13.3 %slice-start = ((s8[4718592]{0:T(1024)(128)(4,1)}), s8[4194304]{0:T(1024)(128)(4,1)S(1)}, s32[]{:S(2)}) async-start(s8[4718592]{0:T(1024)(128)(4,1)} %bitcast.48), calls=%async_computation.8 | async-start | bytes 8388608
  365.2 4.8 slice-start.1
  365.2 7.1 %slice-start.2 = ((s8[4718592]{0:T(1024)(128)(4,1)}), s8[4194304]{0:T(1024)(128)(4,1)S(1)}, s32[]{:S(2)}) async-start(s8[4718592]{0:T(1024)(128)(4,1)} %bitcast.50), calls=%async_computation.10 | async-start | bytes 8388608
  370.1 2.3 slice-start.3
  372.3 8.7 %copy-start.10 = (f32[64,1536]{1,0:T(8,128)S(1)}, f32[64,1536]{1,0:T(8,128)}, u32[]{:S(2)}) copy-start(f32[64,1536]{1,0:T(8,128)} %param.12) | copy-start | bytes 1179652
  382.7 12.1 %copy-start.1 = (bf16[256,1536]{1,0:T(8,128)(2,1)S(1)}, bf16[256,1536]{1,0:T(8,128)(2,1)}, u32[]{:S(2)}) copy-start(bf16[256,1536]{1,0:T(8,128)(2,1)} %convolution_convert_fusion.8.refs_0_) | copy-start | bytes 2359300
  382.7 12.1 %copy-start.2 = (bf16[256,1536]{1,0:T(8,128)(2,1)S(1)}, bf16[256,1536]{1,0:T(8,128)(2,1)}, u32[]{:S(2)}) copy-start(bf16[256,1536]{1,0:T(8,128)(2,1)} %convolution_convert_fusion.7.refs_1_) | copy-start | bytes 2359300
  382.7 12.1 %copy-start.3 = (bf16[256,1536]{1,0:T(8,128)(2,1)S(1)}, bf16[256,1536]{1,0:T(8,128)(2,1)}, u32[]{:S(2)}) copy-start(bf16[256,1536]{1,0:T(8,128)(2,1)} %convolution_convert_fusion.6.refs_2_) | copy-start | bytes 2359300
  532.4 59.8 %reduce-scatter.11.cloned.1.call-start = ((), (), s32[]{:S(2)}) async-start(), calls=%async_computation.7 | async-start | bytes 983040 | tf_op jit(solution)/shard_map/reduce_scatter | solution.py:52
  532.6 7.9 %slice-start.4 = ((s8[4718592]{0:T(1024)(128)(4,1)}), s8[4194304]{0:T(1024)(128)(4,1)S(1)}, s32[]{:S(2)}) async-start(s8[4718592]{0:T(1024)(128)(4,1)} %bitcast.52), calls=%async_computation.12 | async-start | bytes 8388608
  536.5 4.0 slice-start.5
  554.1 24.7 %copy-start.5 = (bf16[256,1536]{1,0:T(8,128)(2,1)S(1)}, bf16[256,1536]{1,0:T(8,128)(2,1)}, u32[]{:S(2)}) copy-start(bf16[256,1536]{1,0:T(8,128)(2,1)} %copy-done.4) | copy-start | bytes 2359300
  578.9 11.5 %copy-start.7 = (f32[64,1536]{1,0:T(8,128)S(1)}, f32[64,1536]{1,0:T(8,128)}, u32[]{:S(2)}) copy-start(f32[64,1536]{1,0:T(8,128)} %param.10) | copy-start | bytes 1179652
  578.9 13.2 %copy-start.8 = (f32[64,1536]{1,0:T(8,128)S(1)}, f32[64,1536]{1,0:T(8,128)}, u32[]{:S(2)}) copy-start(f32[64,1536]{1,0:T(8,128)} %param.13) | copy-start | bytes 1179652
Sparse Core Ops, SparseCore 0:
  332.1 22.8 reduce-scatter.4
  357.7 23.2 reduce-scatter.6
  532.5 21.9 reduce-scatter.8
  557.0 23.2 reduce-scatter.10

commit v2 on v1

--- a/solution.py
+++ b/solution.py
@@ -145,17 +145,21 @@
         rows, cols = ds_of(me, k)
         buf[:, rows, cols] = jnp.zeros((count, rows.size, cols.size), jnp.bfloat16)
 
-    def reduce(k):
-        for j in range(n):
-
-            @pl.when(n - 1 - j > me)
-            def _():
-                hop(right_buf, rs_right, k, n - 1 - j, has_left)
-
-            @pl.when(j < me)
-            def _():
-                hop(left_buf, rs_left, k, j, has_right)
-
+    def hops_right(k):
+        for b in range(n - 1, 0, -1):
+
+            @pl.when(b > me)
+            def _():
+                hop(right_buf, rs_right, k, b, has_left)
+
+    def hops_left(k):
+        for b in range(n - 1):
+
+            @pl.when(b < me)
+            def _():
+                hop(left_buf, rs_left, k, b, has_right)
+
+    def finish(k):
         @pl.when(has_left)
         def _():
             rs_right(k, me).wait_recv()
@@ -183,33 +187,35 @@
         def _():
             ag_left(k, me).start()
 
-    def gather(k):
+    def gather(k, d):
+        @pl.when(me - d >= 0)
+        def _():
+            ag_right(k, me - d).wait_recv()
+
+            @pl.when(has_right)
+            def _():
+                ag_right(k, me - d).start()
+
+        @pl.when(me + d < n)
+        def _():
+            ag_left(k, me + d).wait_recv()
+
+            @pl.when(has_left)
+            def _():
+                ag_left(k, me + d).start()
+
+    def stage(work, k):
+        @pl.when(jnp.logical_and(k >= 0, k < chunks))
+        def _():
+            work(k)
+
+    @pl.loop(0, chunks + 2 * n - 1)
+    def _(t):
+        stage(hops_right, t - me)
+        stage(hops_left, t - (n - 1 - me))
+        stage(finish, t - n)
         for d in range(1, n):
-
-            @pl.when(me - d >= 0)
-            def _():
-                ag_right(k, me - d).wait_recv()
-
-                @pl.when(has_right)
-                def _():
-                    ag_right(k, me - d).start()
-
-            @pl.when(me + d < n)
-            def _():
-                ag_left(k, me + d).wait_recv()
-
-                @pl.when(has_left)
-                def _():
-                    ag_left(k, me + d).start()
-
-    reduce(0)
-
-    @pl.loop(1, chunks)
-    def _(k):
-        reduce(k)
-        gather(k - 1)
-
-    gather(chunks - 1)
+            stage(functools.partial(gather, d=d), t - n - d)
 
     @pl.loop(0, chunks)
     def _(k):
@@ -251,6 +257,34 @@
     )(*arrays)
 
 
+def grad_kernel(left_ref, right_ref, out_ref):
+    out_ref[...] = jnp.dot(
+        left_ref[...], right_ref[...], preferred_element_type=jnp.float32
+    ).astype(jnp.bfloat16)
+
+
+def grad_product(left_t, stacked, index):
+    rows, tokens = left_t.shape
+    width = stacked.shape[2]
+    block = next(b for b in (512, 256, 128, width) if width % b == 0)
+    return pl.pallas_call(
+        grad_kernel,
+        grid=(width // block,),
+        out_shape=jax.ShapeDtypeStruct((rows, width), jnp.bfloat16),
+        in_specs=[
+            pl.BlockSpec((rows, tokens), lambda j: (0, 0)),
+            pl.BlockSpec((None, tokens, block), lambda j: (index, 0, j)),
+        ],
+        out_specs=pl.BlockSpec((rows, block), lambda j: (0, j)),
+        compiler_params=pltpu.CompilerParams(vmem_limit_bytes=24 << 20),
+        cost_estimate=pl.CostEstimate(
+            flops=2 * rows * tokens * width,
+            bytes_accessed=2 * (rows * width + rows * tokens + tokens * width),
+            transcendentals=0,
+        ),
+    )(left_t, stacked)
+
+
 def ffn_middle(ins, right_buf, left_buf, out, rows, cols):
     @pl.loop(0, rows.size // 16)
     def _(r):
@@ -390,7 +424,7 @@
     n_row = lax.axis_size("row")
     pre_term, back_term = for_sending((pre_term, back_term))
     token_rows, hidden_width = pre_term.shape[0] // n_row, pre_term.shape[1]
-    ffn_chunks = max(c for c in (1, 2, 4, 8) if hidden_width % (c * 128) == 0)
+    ffn_chunks = max(c for c in (1, 2, 4, 8, 16) if hidden_width % (c * 128) == 0)
     hidden_slope = chain_exchange(
         n_row,
         (pre_term, back_term),
@@ -401,7 +435,7 @@
     )
     hidden_all, slope_all = hidden_slope[0], hidden_slope[1]
     grad_down = trans_times(hidden_all, grads_all).astype(jnp.bfloat16)
-    grad_up = trans_times(inputs_all, slope_all).astype(jnp.bfloat16)
+    grad_up = grad_product(inputs_all.T, hidden_slope, 1)
     ffn_out, ffn_back = col_totals(
         (
             jnp.dot(hidden_all, w_down, preferred_element_type=jnp.float32),

time: 601 us -> 476 us (0.79)
  Pallas kernels: 402 us -> 294 us
  local copies, waits for them, and re-layouts: 27.5 us -> 8.68 us
  waiting for transfers between devices: 18.2 us -> 36.9 us
  matrix products: 93.5 us -> 77.7 us
    pallas_call x2, Pallas kernels: 402 us -> 283 us  [chain_exchange(): pl.pallas_call(functools.partial(chain_kernel, n, count, chunks, ds_of, m...]
    unnamed x35 -> x42, local copies, waits for them, and re-layouts: 27.5 us -> 8.41 us
    reduce_scatter x2, waiting for transfers between devices: 6.32 us -> 20.3 us  [col_totals(): lax.psum_scatter(arrays[1].astype(jnp.bfloat16), 'col', scatter_dimension...]
    dot_general x2 -> x1, matrix products: 22.6 us -> 9.52 us  [trans_times(): lax.dot_general(first_op, second_op, (((0,), (0,)), ((), ())), preferred_...]
    pallas_call x0 -> x1, Pallas kernels: none -> 11 us  [grad_product(): pl.pallas_call(grad_kernel, grid=(width // block,), out_shape=jax.ShapeDt...]
  transfers between devices with their start and end apart: 4 -> 4, of which waited for: 2 -> 3; matrix products, arithmetic and copies ran while one was open for 14% -> 7% of each run, Pallas kernels for 0% -> 2%
where the time goes in v2:
time: 476 us
  Pallas kernels  294 us (62%)
  matrix products  77.7 us (16%)
  waiting for transfers between devices  36.9 us (8%)
  blocking collectives  35.2 us (7%)
  between operations  14.1 us (3%)
  other arithmetic  9.05 us (2%)
  local copies, waits for them, and re-layouts  8.68 us (2%)
    pallas_call x2, Pallas kernels, chain_exchange(): pl.pallas_call(functools.partial(chain_kernel, n, count, chunks, ds_of, m...  283 us
    dot_general x6, matrix products, times_trans(): lax.dot_general(first_op, second_op, (((1,), (1,)), ((), ())), preferred_...  32.2 us
    reduce_scatter x2, waiting for transfers between devices, col_totals(): lax.psum_scatter(arrays[1].astype(jnp.bfloat16), 'col', scatter_dimension...  20.3 us
    all_gather x2, blocking collectives, col_panels(): lax.all_gather(arrays[1], 'col', axis=0, tiled=True)  18.2 us
    all_gather x2, blocking collectives, col_panels(): lax.all_gather(arrays[0], 'col', axis=0, tiled=True)  16.9 us
    reduce_scatter x2, waiting for transfers between devices, col_totals(): lax.psum_scatter(arrays[0].astype(jnp.bfloat16), 'col', scatter_dimension...  16.6 us
    dot_general x1, matrix products, shards(): pre_term = jnp.dot(inputs_all, w_up, preferred_element_type=jnp.float32)  12.4 us
    dot_general x1, matrix products, shards(): jnp.dot(hidden_all, w_down, preferred_element_type=jnp.float32)  11.1 us
  transfers between devices with their start and end apart: 4, of which 3 were waited for; matrix products, arithmetic and copies ran while one was open for 7% of the time, Pallas kernels for 2%

profile of v2, /device:TPU:0, one launch (start us, length us, event | category | flops | bytes accessed | tf_op | source)
XLA Modules:
  0.0 475.9 jit_solution(8682518726206416684)
XLA Ops:
  9.3 10.0 %all_gather.13 = bf16[256,1536]{1,0:T(8,128)(2,1)S(1)} all-gather(bf16[64,1536]{1,0:T(8,128)(2,1)S(1)} %convert_element_type.59), channel_id=1, replica_groups=mesh['grp'=2,'row'=4,'col'=4] {'col'}, dimensions={0}, use_global_device_ids=true | all-gather | bytes 983040 | tf_op jit(solution)/shard_map/all_gather | solution.py:43
  19.3 8.7 %all_gather.12 = bf16[256,1536]{1,0:T(8,128)(2,1)S(1)} all-gather(bf16[64,1536]{1,0:T(8,128)(2,1)S(1)} %convert_element_type.57), channel_id=1, replica_groups=mesh['grp'=2,'row'=4,'col'=4] {'col'}, dimensions={0}, use_global_device_ids=true | all-gather | bytes 983040 | tf_op jit(solution)/shard_map/all_gather | solution.py:42
  28.9 12.4 %convolution_convert_fusion.2.refs_0_ = bf16[256,6144]{1,0:T(8,128)(2,1)S(1)} fusion(bf16[256,1536]{1,0:T(8,128)(2,1)S(1)} %all_gather.12, bf16[1536,6144]{1,0:T(8,128)(2,1)} %param.18), kind=kOutput, calls=%fused_computation.2 | convolution fusion | flops 4833411072 | bytes 22806528 | tf_op jit(solution)/shard_map/dot_general | solution.py:422
  41.3 10.3 %convolution_convert_fusion.1.refs_1_ = bf16[256,6144]{1,0:T(8,128)(2,1)} fusion(bf16[256,1536]{1,0:T(8,128)(2,1)S(1)} %all_gather.13, bf16[6144,1536]{1,0:T(8,128)(2,1)} %param.19), kind=kOutput, calls=%fused_computation.1 | convolution fusion | flops 4833411072 | bytes 22806528 | tf_op jit(solution)/shard_map/dot_general | solution.py:29
  51.5 1.9 copy-done.2
  53.4 168.0 %shard_map.145.right_ref = bf16[2,256,6144]{2,1,0:T(8,128)(2,1)S(1)} custom-call(bf16[256,6144]{1,0:T(8,128)(2,1)S(1)} %convolution_convert_fusion.2.refs_0_, bf16[256,6144]{1,0:T(8,128)(2,1)S(1)} %copy-done.2), custom_call_target="tpu_custom_call" | custom-call | tf_op jit(solution)/shard_map/pallas_call | solution.py:245
  221.5 2.7 copy-done
  224.2 10.0 %fusion.11 = bf16[256,1536]{1,0:T(8,128)(2,1)} fusion(bf16[1536,6144]{1,0:T(8,128)(2,1)} %param.18, bf16[2,256,6144]{2,1,0:T(8,128)(2,1)S(1)} %shard_map.145.right_ref), kind=kOutput, calls=%fused_computation.14 | convolution fusion | flops 4832231424 | bytes 22806528 | tf_op jit(solution)/shard_map/dot_general | solution.py:29
  234.2 11.1 %fusion.8 = bf16[256,1536]{1,0:T(8,128)(2,1)} fusion(bf16[6144,1536]{1,0:T(8,128)(2,1)} %param.19, bf16[2,256,6144]{2,1,0:T(8,128)(2,1)} %copy-done), kind=kOutput, calls=%fused_computation.13 | convolution fusion | flops 4832231424 | bytes 22806528 | tf_op jit(solution)/shard_map/dot_general | solution.py:441
  245.6 9.8 %reduce-scatter.7.cloned.1.call-done = bf16[64,1536]{1,0:T(8,128)(2,1)} async-done(((bf16[256,1536]{1,0:T(8,128)(2,1)}), bf16[64,1536]{1,0:T(8,128)(2,1)}) %reduce-scatter.7.cloned.1.call-update) | async-done | bytes 196624 | tf_op jit(solution)/shard_map/reduce_scatter | solution.py:52
  257.1 8.2 %all_gather.15 = bf16[256,1536]{1,0:T(8,128)(2,1)S(1)} all-gather(bf16[64,1536]{1,0:T(8,128)(2,1)S(1)} %get-tuple-element.6), channel_id=1, replica_groups=mesh['grp'=2,'row'=4,'col'=4] {'col'}, dimensions={0}, use_global_device_ids=true | all-gather | bytes 983040 | tf_op jit(solution)/shard_map/all_gather | solution.py:43
  265.3 16.6 %reduce-scatter.5.cloned.1.call-done = bf16[64,1536]{1,0:T(8,128)(2,1)} async-done(((bf16[256,1536]{1,0:T(8,128)(2,1)}), bf16[64,1536]{1,0:T(8,128)(2,1)}) %reduce-scatter.5.cloned.1.call-update) | async-done | bytes 196624 | tf_op jit(solution)/shard_map/reduce_scatter | solution.py:49
  283.8 8.2 %all_gather.14 = bf16[256,1536]{1,0:T(8,128)(2,1)S(1)} all-gather(bf16[64,1536]{1,0:T(8,128)(2,1)S(1)} %get-tuple-element.8), channel_id=1, replica_groups=mesh['grp'=2,'row'=4,'col'=4] {'col'}, dimensions={0}, use_global_device_ids=true | all-gather | bytes 983040 | tf_op jit(solution)/shard_map/all_gather | solution.py:42
  292.0 3.8 convolution_convert_fusion.5.refs_2_
  295.8 3.9 convolution_convert_fusion.6.refs_1_
  302.6 114.6 %shard_map.146 = bf16[4,256,1536]{2,1,0:T(8,128)(2,1)} custom-call(bf16[256,1536]{1,0:T(8,128)(2,1)S(1)} %convolution_convert_fusion.7.refs_0_, bf16[256,1536]{1,0:T(8,128)(2,1)S(1)} %convolution_convert_fusion.6.refs_1_, bf16[256,1536]{1,0:T(8,128)(2,1)S(1)} %convolution_convert_fusion.5.refs_2_, bf16[256,1536]{1,0:T(8,128)(2,1)S(1)} %convolution_convert_fusion.4.refs_3_), custom_call_target="tpu_custom_call" | custom-call | tf_op jit(solution)/shard_map/pallas_call | solution.py:245
  417.2 3.5 convolution_convert_fusion.3
  421.4 4.2 fusion.17
  425.6 2.7 convolution_add_fusion.1
  428.4 3.6 fusion.14
  432.1 2.8 copy-done.1
  434.9 11.0 %shard_map.147 = bf16[1536,6144]{1,0:T(8,128)(2,1)} custom-call(bf16[1536,256]{1,0:T(8,128)(2,1)S(1)} %bitcast.46, bf16[2,256,6144]{2,1,0:T(8,128)(2,1)S(1)} %copy-done.1), custom_call_target="tpu_custom_call" | custom-call | flops 4831838208 | bytes 22806528 | tf_op jit(solution)/shard_map/pallas_call | solution.py:270
  446.0 9.5 %convolution_convert_fusion = bf16[6144,1536]{1,0:T(8,128)(2,1)} fusion(bf16[256,1536]{1,0:T(8,128)(2,1)S(1)} %copy-done.6, bf16[2,256,6144]{2,1,0:T(8,128)(2,1)S(1)} %bitcast.45), kind=kOutput, calls=%fused_computation | convolution fusion | flops 4841275392 | bytes 22806528 | tf_op jit(solution)/shard_map/dot_general | solution.py:35
  457.2 10.5 %reduce-scatter.11.cloned.1.call-done = bf16[64,1536]{1,0:T(8,128)(2,1)} async-done(((bf16[256,1536]{1,0:T(8,128)(2,1)}), bf16[64,1536]{1,0:T(8,128)(2,1)}) %reduce-scatter.11.cloned.1.call-update) | async-done | bytes 196624 | tf_op jit(solution)/shard_map/reduce_scatter | solution.py:52
  (62 shorter events, 13.7 us)
Async XLA Ops:
  7.2 248.2 %reduce-scatter.7.cloned.1.call-start = ((), (), s32[]{:S(2)}) async-start(), calls=%async_computation.5 | async-start | bytes 983040 | tf_op jit(solution)/shard_map/reduce_scatter | solution.py:52
  19.3 22.0 %copy-start.5 = (bf16[256,1536]{1,0:T(8,128)(2,1)}, bf16[256,1536]{1,0:T(8,128)(2,1)S(1)}, u32[]{:S(2)}) copy-start(bf16[256,1536]{1,0:T(8,128)(2,1)S(1)} %all_gather.13) | copy-start | bytes 2359300
  51.5 1.9 copy-start.2
  221.5 2.7 copy-start
  234.2 21.2 %copy-start.9 = (f32[64,1536]{1,0:T(8,128)S(1)}, f32[64,1536]{1,0:T(8,128)}, u32[]{:S(2)}) copy-start(f32[64,1536]{1,0:T(8,128)} %param.12) | copy-start | bytes 1179652
  234.2 47.8 %copy-start.10 = (f32[64,1536]{1,0:T(8,128)S(1)}, f32[64,1536]{1,0:T(8,128)}, u32[]{:S(2)}) copy-start(f32[64,1536]{1,0:T(8,128)} %param.11) | copy-start | bytes 1179652
  234.2 47.7 %reduce-scatter.5.cloned.1.call-start = ((), (), s32[]{:S(2)}) async-start(), calls=%async_computation.4 | async-start | bytes 983040 | tf_op jit(solution)/shard_map/reduce_scatter | solution.py:49
  245.4 210.1 %reduce-scatter.9.cloned.1.call-start = ((), (), s32[]{:S(2)}) async-start(), calls=%async_computation.6 | async-start | bytes 983040 | tf_op jit(solution)/shard_map/reduce_scatter | solution.py:49
  281.9 17.8 %slice-start.4 = ((s8[4718592]{0:T(1024)(128)(4,1)}), s8[4194304]{0:T(1024)(128)(4,1)S(1)}, s32[]{:S(2)}) async-start(s8[4718592]{0:T(1024)(128)(4,1)} %bitcast.49), calls=%async_computation.12 | async-start | bytes 8388608
  292.0 7.7 %slice-start.5 = ((s8[4718592]{0:T(1024)(128)(4,1)}), s8[524288]{0:T(1024)(128)(4,1)S(1)}, s32[]{:S(2)}) async-start(s8[4718592]{0:T(1024)(128)(4,1)} %bitcast.49), calls=%async_computation.13 | async-start | bytes 1048576
  295.8 5.3 %slice-start.2 = ((s8[4718592]{0:T(1024)(128)(4,1)}), s8[4194304]{0:T(1024)(128)(4,1)S(1)}, s32[]{:S(2)}) async-start(s8[4718592]{0:T(1024)(128)(4,1)} %bitcast.47), calls=%async_computation.10 | async-start | bytes 8388608
  299.7 1.4 slice-start.3
  417.2 3.8 copy-start.4
  420.8 4.8 %slice-start.6 = ((s8[4718592]{0:T(1024)(128)(4,1)}), s8[524288]{0:T(1024)(128)(4,1)S(1)}, s32[]{:S(2)}) async-start(s8[4718592]{0:T(1024)(128)(4,1)} %bitcast.51), calls=%async_computation.14 | async-start | bytes 1048576
  420.8 46.9 %reduce-scatter.11.cloned.1.call-start = ((), (), s32[]{:S(2)}) async-start(), calls=%async_computation.7 | async-start | bytes 983040 | tf_op jit(solution)/shard_map/reduce_scatter | solution.py:52
  421.3 4.3 slice-start.7
  421.4 7.0 %slice-start.8 = ((s8[4718592]{0:T(1024)(128)(4,1)}), s8[4194304]{0:T(1024)(128)(4,1)S(1)}, s32[]{:S(2)}) async-start(s8[4718592]{0:T(1024)(128)(4,1)} %bitcast.53), calls=%async_computation.16 | async-start | bytes 8388608
  425.6 2.7 slice-start.9
  428.4 17.5 %slice-start = ((s8[6291456]{0:T(1024)(128)(4,1)}), s8[2097152]{0:T(1024)(128)(4,1)S(1)}, s32[]{:S(2)}) async-start(s8[6291456]{0:T(1024)(128)(4,1)} %bitcast.44), calls=%async_computation.8 | async-start | bytes 4194304
  432.0 2.8 copy-start.1
  434.9 11.0 %slice-start.1 = ((s8[6291456]{0:T(1024)(128)(4,1)}), s8[4194304]{0:T(1024)(128)(4,1)S(1)}, s32[]{:S(2)}) async-start(s8[6291456]{0:T(1024)(128)(4,1)} %bitcast.44), calls=%async_computation.9 | async-start | bytes 8388608
  434.9 11.0 %copy-start.6 = (bf16[256,1536]{1,0:T(8,128)(2,1)S(1)}, bf16[256,1536]{1,0:T(8,128)(2,1)}, u32[]{:S(2)}) copy-start(bf16[256,1536]{1,0:T(8,128)(2,1)} %copy-done.5) | copy-start | bytes 2359300
  445.9 9.6 %copy-start.7 = (f32[64,1536]{1,0:T(8,128)S(1)}, f32[64,1536]{1,0:T(8,128)}, u32[]{:S(2)}) copy-start(f32[64,1536]{1,0:T(8,128)} %param.10) | copy-start | bytes 1179652
  445.9 21.7 %copy-start.8 = (f32[64,1536]{1,0:T(8,128)S(1)}, f32[64,1536]{1,0:T(8,128)}, u32[]{:S(2)}) copy-start(f32[64,1536]{1,0:T(8,128)} %param.13) | copy-start | bytes 1179652
  (1 other events, 0.9 us)
Sparse Core Ops, SparseCore 0:
  234.3 21.0 reduce-scatter.6
  258.7 23.2 reduce-scatter.4
  420.9 20.8 reduce-scatter.8
  444.3 23.2 reduce-scatter.10
